TPU v7x, 32 devices: a whole 2x2x4 slice. The times are simulated.
32 devices in a mesh: dom: 4 (over z), ml: 8 (over y, x, core).
Axes of the slice: x: 2, y: 2, z: 4, core: 2. Of those that a mesh axis runs over, the one named last changes fastest.
Arguments:
- mm_positions: float32 [3, 65536], P(None, ('dom', 'ml')), may hold values from -6 to 6
- mm_charge: float32 [65536], P(('dom', 'ml')), may hold values from -1 to 1
- mm_tiles: int32 [512, 8], P(('dom', 'ml')), may hold values from 0 to 47, as said below
- ml_feat: bfloat16 [32, 512, 128], P('dom', 'ml'), may hold values from -6 to 6
- ml_positions: float32 [32, 3, 512], P('dom', None, 'ml'), may hold values from -6 to 6
- ml_neighbours: int32 [32, 32, 512], P('dom', None, 'ml'), may hold values from 0 to 511
- msg_weight: bfloat16 [2, 128, 128], replicated, may hold values from -0.5 to 0.5
- radial_weight: float32 [2, 8, 128], replicated, may hold values from -5 to 5
- out_weight: bfloat16 [2, 128, 128], replicated, may hold values from -0.5 to 0.5
- read_weight: bfloat16 [128, 256], replicated, may hold values from -0.5 to 0.5
Outputs:
- mm_force: float32 [3, 65536], P(None, ('dom', 'ml'))
- ml_force: float32 [32, 3, 512], P('dom', None, 'ml')
Inputs may be any that keep to these rules, and one draw needn't show every extreme that they name: `mm_tiles`: for each tile of a device, 8 distinct positions among the 16 tiles of the previous device along dom+ml (wrapping), its own tiles and the next device's, in that order; at least one lies among the previous device's tiles and at least one among the next device's. `ml_neighbours`: indices of atoms within the same patch.
All inputs are finite; a program needn't handle non-finite values.
Results may differ from a plain program's by a relative error of at most 0.007.
Values may be sent and summed in bfloat16 or wider, within the bound.
A program may use at most 320 MiB of HBM per device.

v0:
```python
import math

import jax
import jax.numpy as jnp
from jax import lax
from jax.sharding import PartitionSpec as P

TILE = 128


RADIUS = 6.0
SOFTEN = 1.0
COULOMB = 0.5


def padded(block, sides, width):
    for axis, dim in sides:
        count = lax.axis_size(axis)
        forward = [(i, i + 1) for i in range(count - 1)]
        forward.append((count - 1, 0))
        backward = [(target, source) for source, target in forward]
        low = lax.ppermute(
            lax.slice_in_dim(block, block.shape[dim] - width, None, axis=dim), axis, forward
        )
        high = lax.ppermute(lax.slice_in_dim(block, 0, width, axis=dim), axis, backward)
        block = jnp.concatenate([low, block, high], axis=dim)
    return block


def pair_force(own_tile, near_tiles):
    offsets = own_tile[:3, None, :, None] - near_tiles[:3, :, None, :]
    squared = jnp.sum(offsets * offsets, axis=0) + SOFTEN
    inverse = 1.0 / (squared * jnp.sqrt(squared))
    strength = COULOMB * own_tile[3][None, :, None] * near_tiles[3][:, None, :] * inverse
    return jnp.sum(strength[None] * offsets, axis=(1, 3))


def slot_forces(
    hidden,
    own_positions,
    neighbours,
    all_positions,
    msg_weight,
    radial_weight,
    out_weight,
    read_weight,
):
    offsets = (
        jax.vmap(lambda table_part, index_part: table_part[:, index_part])(
            all_positions, neighbours
        )
        - own_positions[:, :, None, :]
    )
    distance = jnp.sqrt(jnp.sum(offsets * offsets, axis=1) + 1.0)
    envelope = 0.5 * (jnp.cos(jnp.pi * jnp.minimum(distance / RADIUS, 1.0)) + 1.0)
    basis_count = radial_weight.shape[1]
    centers = jnp.arange(basis_count).astype(jnp.float32) * (RADIUS / basis_count)
    radial_basis = (
        jnp.exp(-2.0 * (distance[:, None] - centers[None, :, None, None]) ** 2) * envelope[:, None]
    )
    norm_factor = 1.0 / math.sqrt(neighbours.shape[1])
    channel_count = hidden.shape[2]
    for layer_index in range(msg_weight.shape[0]):
        mixed_feat = jnp.einsum(
            "rqc,cd->rqd", hidden, msg_weight[layer_index], preferred_element_type=jnp.float32
        ).astype(jnp.bfloat16)
        sender_feat = lax.all_gather(mixed_feat, "ml", axis=1, tiled=True)
        radial_map = radial_weight[layer_index]

        def slot_message(pieces):
            table_part, index_part, basis_part = pieces
            radial = jnp.einsum(
                "nkq,nc->kqc", basis_part, radial_map, precision=lax.Precision.HIGHEST
            )
            return (
                jnp.sum(radial * table_part[index_part].astype(jnp.float32), axis=0) * norm_factor
            )

        message = lax.map(slot_message, (sender_feat, neighbours, radial_basis))
        active = jax.nn.silu(message).astype(jnp.bfloat16)
        update = jnp.einsum(
            "rqc,cd->rqd", active, out_weight[layer_index], preferred_element_type=jnp.float32
        )
        hidden = (hidden.astype(jnp.float32) + update).astype(jnp.bfloat16)
    readout = jnp.einsum(
        "rqc,cd->rqd", hidden, read_weight, preferred_element_type=jnp.float32
    ).astype(jnp.bfloat16)
    query_feat = readout[:, :, :channel_count]
    key_feat = readout[:, :, channel_count:]
    gathered_keys = lax.all_gather(key_feat, "ml", axis=1, tiled=True)

    def slot_pull(pieces):
        query_part, table_part, index_part, envelope_part, offset_part = pieces
        strength = (
            jnp.einsum(
                "qc,kqc->kq", query_part, table_part[index_part], preferred_element_type=jnp.float32
            )
            / channel_count
            * envelope_part
        )
        return jnp.sum(strength[None] * offset_part, axis=1)

    return lax.map(slot_pull, (query_feat, gathered_keys, neighbours, envelope, offsets))


def on_device(
    mm_positions,
    mm_charge,
    mm_tiles,
    ml_feat,
    ml_positions,
    ml_neighbours,
    msg_weight,
    radial_weight,
    out_weight,
    read_weight,
):
    patch_count = ml_feat.shape[0]
    domain_count = lax.axis_size("dom")
    capacity = max(2, 2 * patch_count // domain_count)
    slot_count = domain_count * capacity
    patch_order = jnp.arange(patch_count, dtype=jnp.int32)
    target_group = (
        lax.axis_index("dom") - 1 + patch_order * (domain_count // 2 + 1)
    ) % domain_count
    earlier_same = (target_group[None, :] == target_group[:, None]) & (
        patch_order[None, :] < patch_order[:, None]
    )
    slot_index = target_group * capacity + jnp.sum(earlier_same.astype(jnp.int32), axis=1)
    slot_match = slot_index[None, :] == jnp.arange(slot_count, dtype=jnp.int32)[:, None]
    source = jnp.sum(jnp.where(slot_match, patch_order[None, :], 0), axis=1)
    geometry = jnp.concatenate([ml_positions, ml_neighbours.astype(jnp.float32)], axis=1)
    feat_sent = jnp.take(ml_feat, source, axis=0)
    geometry_sent = jnp.take(geometry, source, axis=0)
    feat_recv = lax.all_to_all(feat_sent, "dom", split_axis=0, concat_axis=0, tiled=True)
    geometry_recv = lax.all_to_all(geometry_sent, "dom", split_axis=0, concat_axis=0, tiled=True)
    mm_atoms = jnp.concatenate([mm_positions, mm_charge[None]], axis=0)
    atom_count = mm_atoms.shape[1]
    tile_count = atom_count // TILE
    window_atoms = padded(mm_atoms, ((("dom", "ml"), 1),), atom_count)
    window_tiles = window_atoms.reshape(4, 3 * tile_count, TILE)
    own_tiles = mm_atoms.reshape(4, tile_count, TILE).transpose(1, 0, 2)

    def tile_force(pieces):
        own_tile, tile_list = pieces
        return pair_force(own_tile, window_tiles[:, tile_list])

    mm_force = lax.map(tile_force, (own_tiles, mm_tiles)).transpose(1, 0, 2).reshape(3, atom_count)
    own_positions = geometry_recv[:, :3]
    all_positions = lax.all_gather(own_positions, "ml", axis=2, tiled=True)
    neighbours = geometry_recv[:, 3:].astype(jnp.int32)
    forces = slot_forces(
        feat_recv,
        own_positions,
        neighbours,
        all_positions,
        msg_weight,
        radial_weight,
        out_weight,
        read_weight,
    )
    returned = lax.all_to_all(forces, "dom", split_axis=0, concat_axis=0, tiled=True)
    ml_force = jnp.take(returned, slot_index, axis=0)
    return (mm_force, ml_force)


def solution(mesh):
    in_specs = (
        P(None, ("dom", "ml")),
        P(("dom", "ml")),
        P(("dom", "ml"), None),
        P("dom", "ml", None),
        P("dom", None, "ml"),
        P("dom", None, "ml"),
        P(),
        P(),
        P(),
        P(),
    )
    out_specs = (P(None, ("dom", "ml")), P("dom", None, "ml"))
    return jax.shard_map(
        on_device, mesh=mesh, in_specs=in_specs, out_specs=out_specs, check_vma=False
    )
```

profile of v0, /device:TPU:0, one launch (start us, length us, event | category | flops | bytes accessed | tf_op | source)
XLA Modules:
  0.0 1133.8 jit_solution(1856930508595932362)
XLA Ops:
  8.8 15.0 %all_to_all.15 = bf16[16,64,128]{2,1,0:T(8,128)(2,1)S(1)} all-to-all(bf16[16,64,128]{2,1,0:T(8,128)(2,1)S(1)} %broadcast_select_fusion), channel_id=1, replica_groups=mesh['dom'=4,'ml'=8] {'dom'}, dimensions={0} | all-to-all | bytes 524288 | tf_op jit(solution)/shard_map/all_to_all | solution.py:135
  38.1 14.2 %all_gather.12 = f32[16,3,512]{0,1,2:T(4,128)S(1)} all-gather(f32[16,3,64]{0,1,2:T(4,128)S(1)} %copy.39), channel_id=1, replica_groups=mesh['dom'=4,'ml'=8] {'ml'}, dimensions={2}, use_global_device_ids=true | all-gather | bytes 110592 | tf_op jit(solution)/shard_map/all_gather | solution.py:150
  57.4 475.1 %gather_fusion.7 = f32[32768,3]{1,0:T(8,128)} fusion(f32[16,3,512]{1,2,0:T(8,128)} %copy.40, s32[32768]{0:T(1024)S(1)} %reshape.355), kind=kCustom, calls=%fused_computation.7 | custom fusion | bytes 1048576 | tf_op jit(solution)/shard_map/vmap()/gather | solution.py:49
  532.5 10.3 copy.41
  547.0 166.0 %while.41 = (s32[]{:T(128)}, f32[16,64,128]{2,1,0:T(8,128)}, f32[16,8,32,64]{3,1,2,0:T(8,128)S(1)}, f32[8,128]{1,0:T(8,128)S(1)}, bf16[16,512,128]{2,1,0:T(8,128)(2,1)}, /*index=5*/s32[16,32,64]{2,1,0:T(8,128)}, s32[]{:T(128)}) while((s32[]{:T(128)}, f32[16,64,128]{2,1,0:T(8,128)}, f32[16,8,32,64]{3,1,2,0:T(8,128)S(1)}, ...), condition=%wide.region_9.10_spmd, body=%wide.region_7.9_spmd.sunk | while | flops 25960448 | bytes 2126425 | solution.py:79
  548.7 6.2 gather_fusion.1
  559.1 6.2 gather_fusion.1
  590.2 6.2 gather_fusion.1
  610.9 6.2 gather_fusion.1
  621.3 6.2 gather_fusion.1
  631.7 6.2 gather_fusion.1
  642.1 6.2 gather_fusion.1
  652.4 6.2 gather_fusion.1
  662.8 6.2 gather_fusion.1
  673.2 6.2 gather_fusion.1
  683.6 6.2 gather_fusion.1
  693.9 6.2 gather_fusion.1
  704.3 6.2 gather_fusion.1
  715.3 26.3 %all-gather.6.cloned.1.call-done = bf16[16,512,128]{2,1,0:T(8,128)(2,1)} async-done(((bf16[16,64,128]{2,1,0:T(8,128)(2,1)}), bf16[16,512,128]{2,1,0:T(8,128)(2,1)}) %all-gather.6.cloned.1.call-update) | async-done | bytes 2097168 | tf_op jit(solution)/shard_map/all_gather | solution.py:67
  742.4 165.9 %while.42 = (s32[]{:T(128)}, f32[16,64,128]{2,1,0:T(8,128)}, f32[16,8,32,64]{3,1,2,0:T(8,128)S(1)}, f32[8,128]{1,0:T(8,128)S(1)}, bf16[16,512,128]{2,1,0:T(8,128)(2,1)}, /*index=5*/s32[16,32,64]{2,1,0:T(8,128)}, s32[]{:T(128)}) while((s32[]{:T(128)}, f32[16,64,128]{2,1,0:T(8,128)}, f32[16,8,32,64]{3,1,2,0:T(8,128)S(1)}, ...), condition=%wide.region_12.13_spmd, body=%wide.region_10.12_spmd.sunk | while | flops 25960448 | bytes 2126425 | solution.py:79
  754.5 6.2 gather_fusion.2
  785.6 6.2 gather_fusion.2
  806.4 6.2 gather_fusion.2
  816.7 6.2 gather_fusion.2
  827.1 6.2 gather_fusion.2
  837.5 6.2 gather_fusion.2
  847.9 6.2 gather_fusion.2
  858.2 6.2 gather_fusion.2
  868.6 6.2 gather_fusion.2
  879.0 6.2 gather_fusion.2
  889.3 6.2 gather_fusion.2
  899.7 6.2 gather_fusion.2
  917.9 21.0 %all-gather.8.cloned.1.call-done = bf16[16,512,128]{2,1,0:T(8,128)(2,1)} async-done(((bf16[16,64,128]{2,1,0:T(8,128)(2,1)}), bf16[16,512,128]{2,1,0:T(8,128)(2,1)}) %all-gather.8.cloned.1.call-update) | async-done | bytes 2097168 | tf_op jit(solution)/shard_map/all_gather | solution.py:90
  938.8 148.7 %while.43 = (s32[]{:T(128)}, f32[16,3,64]{2,1,0:T(4,128)S(1)}, bf16[16,512,128]{2,1,0:T(8,128)(2,1)}, s32[16,32,64]{2,1,0:T(8,128)}, bf16[16,64,128]{2,1,0:T(8,1...) while((s32[]{:T(128)}, f32[16,3,64]{2,1,0:T(4,128)S(1)}, ...), condition=%wide.region_15.16_spmd, body=%wide.region_13.15_spmd.sunk | while | flops 548674 | bytes 2028397 | solution.py:103
  940.6 6.2 gather_fusion.3
  949.9 6.2 gather_fusion.3
  977.7 6.2 gather_fusion.3
  996.3 6.2 gather_fusion.3
  1005.6 6.2 gather_fusion.3
  1014.9 6.2 gather_fusion.3
  1024.2 6.2 gather_fusion.3
  1033.5 6.2 gather_fusion.3
  1042.8 6.2 gather_fusion.3
  1052.1 6.2 gather_fusion.3
  1061.4 6.2 gather_fusion.3
  1070.7 6.2 gather_fusion.3
  1079.9 6.2 gather_fusion.3
  1092.8 32.5 %while.40 = (s32[]{:T(128)}, f32[16,3,128]{2,1,0:T(4,128)}, f32[16,4,128]{2,1,0:T(4,128)S(1)}, s32[16,8]{1,0:T(8,128)S(1)}, f32[4,48,128]{2,0,1:T(4,128)S(1)}, /*index=5*/s32[]{:T(128)}) while((s32[]{:T(128)}, f32[16,3,128]{2,1,0:T(4,128)}, f32[16,4,128]{2,1,0:T(4,128)S(1)}, s32[16,8]{1,0:T(8,128)S(1)}, f32[4,48,128]{2,0,1:T(4,128)S(1)}, ...), condition=%wide.region_3.4_spmd, body=%wide.region_0.0_spmd.sunk | while | flops 2884378 | bytes 2213069 | solution.py:148
  (635 shorter events, 320.8 us)
Async XLA Ops:
  7.2 0.9 copy-start
  7.2 18.3 %copy-start.2 = (s32[8,32,64]{2,1,0:T(8,128)S(1)}, s32[8,32,64]{2,1,0:T(8,128)}, u32[]{:S(2)}) copy-start(s32[8,32,64]{2,1,0:T(8,128)} %param.23) | copy-start | bytes 196612
  7.2 18.3 %copy-start.5 = (f32[8,3,64]{2,0,1:T(8,128)S(1)}, f32[8,3,64]{2,0,1:T(8,128)}, u32[]{:S(2)}) copy-start(f32[8,3,64]{2,0,1:T(8,128)} %param.22) | copy-start | bytes 18436
  7.2 538.9 %all-gather.4.cloned.1.call-start = ((), (), s32[]{:S(2)}) async-start(), calls=%async_computation.3 | async-start | bytes 2359296 | tf_op jit(solution)/shard_map/all_gather | solution.py:67
  8.8 21.7 %copy-start.6 = (f32[2,8,128]{2,1,0:T(8,128)S(1)}, f32[2,8,128]{2,1,0:T(8,128)}, u32[]{:S(2)}) copy-start(f32[2,8,128]{2,1,0:T(8,128)} %param.25) | copy-start | bytes 24580
  27.1 9.3 all-to-all-start.1
  30.4 711.2 %all-gather.6.cloned.1.call-start = ((), (), s32[]{:S(2)}) async-start(), calls=%async_computation.4 | async-start | bytes 2359296 | tf_op jit(solution)/shard_map/all_gather | solution.py:67
  712.9 1.4 copy-start.4
  715.3 223.6 %all-gather.8.cloned.1.call-start = ((), (), s32[]{:S(2)}) async-start(), calls=%async_computation.5 | async-start | bytes 2359296 | tf_op jit(solution)/shard_map/all_gather | solution.py:90
  908.4 2.4 copy-start.1
  908.4 2.4 copy-start.3
  908.4 7.9 copy-start.7
  910.8 7.0 collective-permute-start
  911.1 6.7 collective-permute-start.1
  1088.2 37.1 %all-to-all-start.2 = ((f32[4,1,768]{2,1,0:T(1,128)}), f32[4,1,768]{2,1,0:T(1,128)S(1)}, u32[]{:S(2)}, u32[]{:S(2)}) async-start(f32[4,1,768]{2,1,0:T(1,128)} %reshape.382), calls=%async_computation.2 | async-start | bytes 24576 | tf_op jit(solution)/shard_map/all_to_all | solution.py:162
Sparse Core Ops, SparseCore 0:
  25.6 29.5 all-gather.3
  715.4 26.1 all-gather.5
  910.9 27.8 all-gather.7
where the time goes:
time: 1140 us; the launch traced here: 1130 us
  local copies, waits for them, and re-layouts  863 us (76%)
  other arithmetic  86.8 us (8%)
  matrix products  70.8 us (6%)
  waiting for transfers between devices  54.6 us (5%)
  blocking collectives  29.2 us (3%)
  between operations  14.1 us (1%)
  starting transfers between devices  13.5 us (1%)
    gather x3, local copies, waits for them, and re-layouts, slot_forces(): table_part[:, index_part]  486 us
    gather x32, local copies, waits for them, and re-layouts, slot_message(): table_part[index_part].astype(jnp.float32)  198 us
    gather x16, local copies, waits for them, and re-layouts, slot_pull(): table_part[index_part]  98.8 us
    dot_general x32, matrix products, slot_message(): jnp.einsum('nkq,nc->kqc', basis_part, radial_map, precision=lax.Precision...  58.7 us
    squeeze x48, local copies, waits for them, and re-layouts, slot_forces(): message = lax.map(slot_message, (sender_feat, neighbours, radial_basis))  43.9 us
    all_gather x2, waiting for transfers between devices, slot_forces(): sender_feat = lax.all_gather(mixed_feat, 'ml', axis=1, tiled=True)  26.3 us
    select_n x32, other arithmetic, slot_message(): table_part[index_part].astype(jnp.float32)  23.3 us
  transfers between devices with their start and end apart: 7, of which 4 were waited for; matrix products, arithmetic and copies ran while one was open for 47% of the time, Pallas kernels for 0%

commit v1 on v0

v1 whole, which is shorter than its diff:
```python
import functools
import math

import jax
import jax.numpy as jnp
from jax import lax
from jax.experimental import pallas as pl
from jax.experimental.pallas import tpu as pltpu
from jax.sharding import PartitionSpec as P

TILE = 128
RADIUS = 6.0
SOFTEN = 1.0
COULOMB = 0.5
F32 = jnp.float32
BF16 = jnp.bfloat16
MESH = pl.DeviceIdType.MESH
ANY = pl.BlockSpec(memory_space=pl.ANY)
VMEM = pl.BlockSpec(memory_space=pltpu.VMEM)


def split3(x):
    high = x.astype(BF16).astype(F32)
    rest = x - high
    middle = rest.astype(BF16).astype(F32)
    return high, middle, (rest - middle).astype(BF16).astype(F32)


def last_row(shape):
    return lax.broadcasted_iota(jnp.int32, shape, 0) == 3


def left_factor(xyz):
    norm = jnp.sum(xyz * xyz, axis=0, keepdims=True)
    high, middle, low = split3(jnp.concatenate([xyz, norm], axis=0))
    last = last_row(high.shape)
    one = jnp.ones_like(high)
    groups = [
        high,
        jnp.where(last, middle, high),
        jnp.where(last, low, middle),
        jnp.where(last, one, high),
        jnp.where(last, one, low),
        jnp.where(last, one, middle),
        jnp.zeros_like(high),
        jnp.zeros_like(high),
    ]
    return jnp.concatenate(groups, axis=0)


def right_factor(xyz):
    norm = jnp.sum(xyz * xyz, axis=0, keepdims=True) + SOFTEN
    high, middle, low = split3(jnp.concatenate([-2.0 * xyz, norm], axis=0))
    last = last_row(high.shape)
    one = jnp.ones_like(high)
    groups = [
        jnp.where(last, one, high),
        jnp.where(last, one, middle),
        jnp.where(last, one, high),
        low,
        high,
        middle,
        jnp.zeros_like(high),
        jnp.zeros_like(high),
    ]
    return jnp.concatenate(groups, axis=0).astype(BF16)


def moment_rows(xyz, weight):
    rows = jnp.concatenate([xyz * weight, weight], axis=0)
    high, middle, low = split3(rows)
    return jnp.concatenate([high, middle, low, jnp.zeros_like(high)], axis=0).astype(BF16)


def folded(moments):
    return moments[0:4] + moments[4:8] + moments[8:12]


def dot(a, b):
    return jnp.dot(a, b, preferred_element_type=F32)


def half_wave(u):
    x = u * (math.pi / 2)
    y = x * x
    p = -1.0 / 39916800
    for c in (1.0 / 362880, -1.0 / 5040, 1.0 / 120, -1.0 / 6, 1.0):
        p = p * y + c
    return p * x


def kernel(
    shape,
    mm_pos,
    mm_charge,
    mm_tiles,
    feat,
    pos,
    nbr,
    msg_w,
    rad_w,
    out_w,
    read_w,
    mm_out,
    ml_out,
    win_p,
    win_q,
    tiles,
    feat_buf,
    pos_buf,
    nbr_buf,
    msg_v,
    rad_v,
    out_v,
    read_v,
    near_v,
    near_r,
    own_u,
    word_s,
    value_s,
    basis,
    weight_s,
    rad_cols,
    stage,
    force_buf,
    local_sem,
    halo_send,
    halo_recv,
    ml_send,
    ml_recv,
    back_send,
    back_recv,
):
    doms, mls = shape
    patches = feat.shape[0]
    atoms = feat.shape[1]
    nbrs = nbr.shape[1]
    psize = mls * atoms
    layers, nb, width = rad_w.shape
    tile_nbrs, tile_count = mm_tiles.shape

    dom = lax.axis_index("dom")
    me = lax.axis_index("ml")
    flat = dom * mls + me
    after = lax.rem(flat + 1, doms * mls)
    before = lax.rem(flat + doms * mls - 1, doms * mls)
    sides = [(before // mls, lax.rem(before, mls)), (after // mls, lax.rem(after, mls))]
    my_patch = lax.rem(me, patches)

    local = [
        pltpu.make_async_copy(mm_pos, win_p.at[1], local_sem.at[0]),
        pltpu.make_async_copy(mm_charge, win_q.at[1], local_sem.at[1]),
        pltpu.make_async_copy(mm_tiles, tiles, local_sem.at[2]),
        pltpu.make_async_copy(msg_w, msg_v, local_sem.at[3]),
        pltpu.make_async_copy(rad_w, rad_v, local_sem.at[4]),
        pltpu.make_async_copy(out_w, out_v, local_sem.at[5]),
        pltpu.make_async_copy(read_w, read_v, local_sem.at[6]),
        pltpu.make_async_copy(nbr.at[my_patch], nbr_buf.at[me], local_sem.at[7]),
        pltpu.make_async_copy(pos, pos_buf.at[me], local_sem.at[8]),
        pltpu.make_async_copy(feat.at[my_patch], feat_buf.at[me], local_sem.at[9]),
    ]
    for copy in local:
        copy.start()

    barrier = pltpu.get_barrier_semaphore()
    for side in sides:
        pl.semaphore_signal(barrier, inc=1, device_id=side, device_id_type=MESH)
    peers = [lax.rem(me + o, mls) for o in range(1, mls)]
    for peer in peers:
        pl.semaphore_signal(barrier, inc=1, device_id=(dom, peer), device_id_type=MESH)
    pl.semaphore_wait(barrier, mls + 1)

    halo = []
    for k, (side, slab) in enumerate(zip(sides, (2, 0))):
        for m, (src, dst) in enumerate(((mm_pos, win_p), (mm_charge, win_q))):
            halo.append(
                pltpu.make_async_remote_copy(
                    src_ref=src,
                    dst_ref=dst.at[slab],
                    send_sem=halo_send.at[2 * k + m],
                    recv_sem=halo_recv.at[2 * k + m],
                    device_id=side,
                    device_id_type=MESH,
                )
            )
    for copy in halo:
        copy.start()
    moves = []
    for m, (src, dst) in enumerate(((nbr, nbr_buf), (pos, pos_buf), (feat, feat_buf))):
        group = []
        for o, peer in enumerate(peers):
            group.append(
                pltpu.make_async_remote_copy(
                    src_ref=src if m == 1 else src.at[lax.rem(peer, patches)],
                    dst_ref=dst.at[me],
                    send_sem=ml_send.at[m, o],
                    recv_sem=ml_recv.at[m, o],
                    device_id=(dom, peer),
                    device_id_type=MESH,
                )
            )
        for copy in group:
            copy.start()
        moves.append(group)

    for copy in local:
        copy.wait()
    center = nb // 2
    step = RADIUS / nb
    factors = [
        math.exp(-2.0 * (step * (n - center)) ** 2) / math.sqrt(nbrs) for n in range(nb)
    ]
    for l in range(layers):
        columns = jnp.concatenate([rad_v[l], jnp.zeros((width - nb, width), F32)], axis=0).T
        for n in range(nb):
            rad_cols[l, n] = jnp.broadcast_to(columns[:, n : n + 1] * factors[n], (width, TILE))
    left = left_factor(win_p[1])
    for t in range(tile_count):
        own_u[t] = left[:, t * TILE : (t + 1) * TILE].T.astype(BF16)

    def near_slab(slab):
        xyz = win_p[slab]
        right = right_factor(xyz)
        rows = moment_rows(xyz, win_q[slab])
        for t in range(tile_count):
            near_v[slab * tile_count + t] = right[:, t * TILE : (t + 1) * TILE]
            near_r[slab * tile_count + t] = rows[:, t * TILE : (t + 1) * TILE]

    near_slab(1)
    for copy in halo:
        copy.wait_recv()
    near_slab(0)
    near_slab(2)

    def mm_tile(t, carry):
        own = own_u[t]
        total = jnp.zeros((16, TILE), F32)
        for c in range(0, tile_nbrs, 2):
            one, two = tiles[c, t], tiles[c + 1, t]
            right = jnp.concatenate([near_v[one], near_v[two]], axis=1)
            rows = jnp.concatenate([near_r[one], near_r[two]], axis=1)
            inverse = lax.rsqrt(dot(own, right))
            cubed = (inverse * inverse * inverse).astype(BF16)
            total = total + lax.dot_general(
                rows, cubed, (((1,), (1,)), ((), ())), preferred_element_type=F32
            )
        at = pl.ds(pl.multiple_of(t * TILE, TILE), TILE)
        sums = folded(total)
        force = win_p[1, :, at] * sums[3:4] - sums[0:3]
        mm_out[:, at] = force * (COULOMB * win_q[1, :, at])
        return carry

    first_half = tile_count // 2
    lax.fori_loop(0, first_half, mm_tile, 0)

    for copy in moves[0] + moves[1]:
        copy.wait_recv()
    listed = jnp.concatenate([nbr_buf[d] for d in range(mls)], axis=1)
    words = psize // 4
    word_s[...] = lax.rem(listed, words)
    value_s[...] = jnp.left_shift(1, 8 * (listed // words))
    xyz = jnp.concatenate([pos_buf[d, :, my_patch, :] for d in range(mls)], axis=1)
    senders = left_factor(xyz).T.astype(BF16)
    receivers = right_factor(xyz)
    rows = moment_rows(xyz, jnp.ones_like(xyz[0:1]))
    for ib in range(psize // TILE):
        at = slice(ib * TILE, (ib + 1) * TILE)
        place = lax.broadcasted_iota(jnp.int32, (words, TILE), 0)
        counts = jnp.zeros((words, TILE), jnp.int32)
        for k in range(nbrs):
            hit = place == word_s[k : k + 1, at]
            counts = counts + jnp.where(hit, value_s[k : k + 1, at], 0)
        for b in range(4):
            rows_at = slice(b * words, (b + 1) * words)
            count = (jnp.right_shift(counts, 8 * b) & 255).astype(F32)
            squared = dot(senders[rows_at], receivers[:, at])
            distance = jnp.minimum(squared * lax.rsqrt(squared), RADIUS)
            wave = half_wave(1.0 - distance * (1.0 / RADIUS))
            weight = count * (wave * wave)
            weight_s[rows_at, at] = weight
            shifted = distance - center * step
            middle = weight * jnp.exp(-2.0 * shifted * shifted)
            basis[center, rows_at, at] = middle.astype(BF16)
            up = jnp.exp(4.0 * step * shifted)
            value = middle
            for n in range(center + 1, nb):
                value = value * up
                basis[n, rows_at, at] = value.astype(BF16)
            down = jnp.exp(-4.0 * step * shifted)
            value = middle
            for n in range(center - 1, -1, -1):
                value = value * down
                basis[n, rows_at, at] = value.astype(BF16)

    for copy in moves[2]:
        copy.wait_recv()
    hidden = feat_buf[...].reshape(psize, width).astype(F32).T.astype(BF16)
    for l in range(layers):
        mixed = dot(msg_v[l].astype(F32).T.astype(BF16), hidden).astype(BF16)
        message = jnp.zeros((width, psize), F32)
        for n in range(nb):
            column = jnp.concatenate([rad_cols[l, n]] * (psize // TILE), axis=1)
            message = message + column * dot(mixed, basis[n])
        active = (message / (1.0 + jnp.exp(-message))).astype(BF16)
        update = dot(out_v[l].astype(F32).T.astype(BF16), active)
        hidden = (hidden.astype(F32) + update).astype(BF16)
    readout = dot(read_v[...].astype(F32).T.astype(BF16), hidden)
    query = readout[:width].astype(BF16)
    key = readout[width:].T.astype(BF16)
    strength = dot(key, query) * weight_s[...] * (1.0 / width)
    strong = strength.astype(BF16)
    weak = (strength - strong.astype(F32)).astype(BF16)
    sums = folded(dot(rows, strong) + dot(rows, weak))
    force = sums[0:3] - xyz * sums[3:4]
    for d in range(mls):
        stage[d] = force[:, d * atoms : (d + 1) * atoms]
    group = me - my_patch
    returns = []
    for o in range(1, patches):
        owner = group + lax.rem(my_patch + o, patches)
        copy = pltpu.make_async_remote_copy(
            src_ref=stage.at[owner],
            dst_ref=force_buf.at[my_patch],
            send_sem=back_send.at[o - 1],
            recv_sem=back_recv.at[o - 1],
            device_id=(dom, owner),
            device_id_type=MESH,
        )
        copy.start()
        returns.append(copy)
    own = pltpu.make_async_copy(stage.at[me], force_buf.at[my_patch], local_sem.at[0])
    own.start()

    lax.fori_loop(first_half, tile_count, mm_tile, 0)

    for copy in halo:
        copy.wait_send()
    for group in moves:
        for copy in group:
            copy.wait_send()
    own.wait()
    for copy in returns:
        copy.wait()
    for p in range(patches):
        ml_out[:, p, :] = force_buf[p]


def on_device(
    shape,
    mm_positions,
    mm_charge,
    mm_tiles,
    ml_feat,
    ml_positions,
    ml_neighbours,
    msg_weight,
    radial_weight,
    out_weight,
    read_weight,
):
    mls = shape[1]
    patches, atoms, width = ml_feat.shape
    nbrs = ml_neighbours.shape[1]
    psize = mls * atoms
    layers, nb, _ = radial_weight.shape
    count = mm_positions.shape[1]
    tile_count = count // TILE
    dma = pltpu.SemaphoreType.DMA
    mm_force, ml_force = pl.pallas_call(
        functools.partial(kernel, shape),
        out_shape=(
            jax.ShapeDtypeStruct((3, count), F32),
            jax.ShapeDtypeStruct((3, patches, atoms), F32),
        ),
        in_specs=[ANY] * 10,
        out_specs=(VMEM, VMEM),
        scratch_shapes=[
            pltpu.VMEM((3, 3, count), F32),
            pltpu.VMEM((3, 1, count), F32),
            pltpu.SMEM(mm_tiles.shape[::-1], jnp.int32),
            pltpu.VMEM((mls, atoms, width), BF16),
            pltpu.VMEM((mls, 3, patches, atoms), F32),
            pltpu.VMEM((mls, nbrs, atoms), jnp.int32),
            pltpu.VMEM(msg_weight.shape, BF16),
            pltpu.VMEM(radial_weight.shape, F32),
            pltpu.VMEM(out_weight.shape, BF16),
            pltpu.VMEM(read_weight.shape, BF16),
            pltpu.VMEM((3 * tile_count, 32, TILE), BF16),
            pltpu.VMEM((3 * tile_count, 16, TILE), BF16),
            pltpu.VMEM((tile_count, TILE, 32), BF16),
            pltpu.VMEM((nbrs, psize), jnp.int32),
            pltpu.VMEM((nbrs, psize), jnp.int32),
            pltpu.VMEM((nb, psize, psize), BF16),
            pltpu.VMEM((psize, psize), F32),
            pltpu.VMEM((layers, nb, width, TILE), F32),
            pltpu.VMEM((mls, 3, atoms), F32),
            pltpu.VMEM((patches, 3, atoms), F32),
            dma((10,)),
            dma((4,)),
            dma((4,)),
            dma((3, mls)),
            dma((3, mls)),
            dma((patches,)),
            dma((patches,)),
        ],
        compiler_params=pltpu.CompilerParams(
            collective_id=0, has_side_effects=True, vmem_limit_bytes=60 * 1024 * 1024
        ),
        name="force_step",
    )(
        mm_positions,
        mm_charge.reshape(1, count),
        mm_tiles.T,
        ml_feat,
        ml_positions.transpose(1, 0, 2),
        ml_neighbours,
        msg_weight,
        radial_weight,
        out_weight,
        read_weight,
    )
    return mm_force, ml_force.transpose(1, 0, 2)


def solution(mesh):
    shape = (mesh.shape["dom"], mesh.shape["ml"])
    in_specs = (
        P(None, ("dom", "ml")),
        P(("dom", "ml")),
        P(("dom", "ml"), None),
        P("dom", "ml", None),
        P("dom", None, "ml"),
        P("dom", None, "ml"),
        P(),
        P(),
        P(),
        P(),
    )
    out_specs = (P(None, ("dom", "ml")), P("dom", None, "ml"))
    return jax.shard_map(
        functools.partial(on_device, shape),
        mesh=mesh,
        in_specs=in_specs,
        out_specs=out_specs,
        check_vma=False,
    )
```

time: 1140 us -> 28.1 us (0.02)
  local copies, waits for them, and re-layouts: 863 us -> 1.99 us
  other arithmetic: 86.8 us -> 0 us
  matrix products: 70.8 us -> 0 us
  waiting for transfers between devices: 54.6 us -> 0 us
  blocking collectives: 29.2 us -> 0 us
  Pallas kernels: 0 us -> 25.2 us
  starting transfers between devices: 13.5 us -> 0 us
  between operations: 14.1 us -> 0.65 us
    gather x70 -> x0, local copies, waits for them, and re-layouts: 793 us -> none  [the longest x3 486 us: slot_forces(): table_part[:, index_part]]
    dot_general x52 -> x0, matrix products: 70.8 us -> none  [the longest x32 58.7 us: slot_message(): jnp.einsum('nkq,nc->kqc', basis_part, radial_map, precision=lax.Precision...]
    all_gather x3 -> x0, waiting for transfers between devices: 47.2 us -> none  [the longest x2 26.3 us: slot_forces(): sender_feat = lax.all_gather(mixed_feat, 'ml', axis=1, tiled=True)]
    squeeze x65 -> x0, local copies, waits for them, and re-layouts: 44 us -> none  [the longest x48 43.9 us: slot_forces(): message = lax.map(slot_message, (sender_feat, neighbours, radial_basis))]
    select_n x70 -> x0, other arithmetic: 35.3 us -> none  [the longest x32 23.3 us: slot_message(): table_part[index_part].astype(jnp.float32)]
    pallas_call x0 -> x1, Pallas kernels: none -> 25.2 us  [on_device(): pl.pallas_call(functools.partial(kernel, shape), out_shape=(jax.ShapeDtyp...]
    reduce_sum x51 -> x0, other arithmetic: 23.1 us -> none  [the longest x16 13.3 us: slot_pull(): return jnp.sum(strength[None] * offset_part, axis=1)]
    dynamic_update_slice x32 -> x0, other arithmetic: 19.8 us -> none  [slot_forces(): message = lax.map(slot_message, (sender_feat, neighbours, radial_basis))]
  transfers between devices with their start and end apart: 7 -> 0, of which waited for: 4 -> 0; matrix products, arithmetic and copies ran while one was open for 47% -> 0% of each run, Pallas kernels for 0% -> 0%
where the time goes in v1:
time: 28.1 us; the launch traced here: 27.9 us
  Pallas kernels  25.2 us (90%)
  local copies, waits for them, and re-layouts  1.99 us (7%)
  between operations  0.65 us (2%)
    pallas_call x1, Pallas kernels, on_device(): pl.pallas_call(functools.partial(kernel, shape), out_shape=(jax.ShapeDtyp...  25.2 us
    unnamed x4, local copies, waits for them, and re-layouts  1.99 us

profile of v1, /device:TPU:0, one launch (start us, length us, event | category | flops | bytes accessed | tf_op | source)
XLA Modules:
  0.0 27.9 jit_solution(16179058773871804340)
XLA Ops:
  0.6 25.2 %force_step.1 = (f32[3,2048]{1,0:T(4,128)}, f32[3,8,64]{2,1,0:T(8,128)}) custom-call(f32[3,2048]{1,0:T(4,128)} %mm_pos.1, f32[1,2048]{1,0:T(1,128)} %bitcast.6, s32[8,16]{1,0:T(8,128)} %bitcast.7, bf16[8,64,128]{2,1,0:T(8,128)(2,1)} %feat.1, f32[3,8,64]{2,1,0:T(8,128)} %bitcast.5, s32[8,32,64]{2,1,0:T(8,128)} %nbr.1, bf16[2,128,128]{2,1,0:T(8,128)(2,1)} %msg_w.1, ...), custom_call_target="tpu_custom_call" | custom-call | tf_op jit(solution)/shard_map/force_step/pallas_call | solution.py:369
  25.9 0.0 copy-start
  25.9 1.4 %copy.14 = f32[3,2048]{1,0:T(4,128)} copy(f32[3,2048]{1,0:T(4,128)} %get-tuple-element.8) | data formatting | bytes 49152
  27.3 0.0 copy-done
  27.3 0.6 %copy.15 = f32[8,3,64]{2,0,1:T(8,128)} copy(f32[8,3,64]{2,0,1:T(8,128)S(1)} %bitcast.4) | data formatting | bytes 12288
Async XLA Ops:
  25.9 1.4 %copy-start = (f32[3,8,64]{2,1,0:T(8,128)S(1)}, f32[3,8,64]{2,1,0:T(8,128)}, u32[]{:S(2)}) copy-start(f32[3,8,64]{2,1,0:T(8,128)} %get-tuple-element.5) | copy-start | bytes 18436

commit v2 on v1

--- a/solution.py
+++ b/solution.py
@@ -12,6 +12,7 @@
 RADIUS = 6.0
 SOFTEN = 1.0
 COULOMB = 0.5
+CHUNK = 32
 F32 = jnp.float32
 BF16 = jnp.bfloat16
 MESH = pl.DeviceIdType.MESH
@@ -118,7 +119,9 @@
     own_u,
     word_s,
     value_s,
+    count_s,
     basis,
+    spread,
     weight_s,
     rad_cols,
     stage,
@@ -251,7 +254,7 @@
         return carry
 
     first_half = tile_count // 2
-    lax.fori_loop(0, first_half, mm_tile, 0)
+    lax.fori_loop(0, first_half, mm_tile, 0, unroll=True)
 
     for copy in moves[0] + moves[1]:
         copy.wait_recv()
@@ -270,37 +273,42 @@
         for k in range(nbrs):
             hit = place == word_s[k : k + 1, at]
             counts = counts + jnp.where(hit, value_s[k : k + 1, at], 0)
+        count_s[...] = counts
         for b in range(4):
-            rows_at = slice(b * words, (b + 1) * words)
-            count = (jnp.right_shift(counts, 8 * b) & 255).astype(F32)
-            squared = dot(senders[rows_at], receivers[:, at])
-            distance = jnp.minimum(squared * lax.rsqrt(squared), RADIUS)
-            wave = half_wave(1.0 - distance * (1.0 / RADIUS))
-            weight = count * (wave * wave)
-            weight_s[rows_at, at] = weight
-            shifted = distance - center * step
-            middle = weight * jnp.exp(-2.0 * shifted * shifted)
-            basis[center, rows_at, at] = middle.astype(BF16)
-            up = jnp.exp(4.0 * step * shifted)
-            value = middle
-            for n in range(center + 1, nb):
-                value = value * up
-                basis[n, rows_at, at] = value.astype(BF16)
-            down = jnp.exp(-4.0 * step * shifted)
-            value = middle
-            for n in range(center - 1, -1, -1):
-                value = value * down
-                basis[n, rows_at, at] = value.astype(BF16)
+            for c in range(0, words, CHUNK):
+                row = b * words + c
+                rows_at = slice(row, row + CHUNK)
+                count = (jnp.right_shift(count_s[c : c + CHUNK], 8 * b) & 255).astype(F32)
+                squared = dot(senders[rows_at], receivers[:, at])
+                distance = jnp.minimum(squared * lax.rsqrt(squared), RADIUS)
+                wave = half_wave(1.0 - distance * (1.0 / RADIUS))
+                weight = count * (wave * wave)
+                weight_s[rows_at, at] = weight
+                shifted = distance - center * step
+                scaled = shifted * (4.0 * step / math.log(2.0))
+                middle = weight * jnp.exp2(shifted * shifted * (-2.0 / math.log(2.0)))
+                up = jnp.exp2(scaled)
+                down = jnp.exp2(-scaled)
+                basis[center * psize + row : center * psize + row + CHUNK, at] = middle.astype(BF16)
+                value = middle
+                for n in range(center + 1, nb):
+                    value = value * up
+                    basis[n * psize + row : n * psize + row + CHUNK, at] = value.astype(BF16)
+                value = middle
+                for n in range(center - 1, -1, -1):
+                    value = value * down
+                    basis[n * psize + row : n * psize + row + CHUNK, at] = value.astype(BF16)
 
     for copy in moves[2]:
         copy.wait_recv()
     hidden = feat_buf[...].reshape(psize, width).astype(F32).T.astype(BF16)
     for l in range(layers):
         mixed = dot(msg_v[l].astype(F32).T.astype(BF16), hidden).astype(BF16)
-        message = jnp.zeros((width, psize), F32)
+        wide = mixed.astype(F32)
         for n in range(nb):
             column = jnp.concatenate([rad_cols[l, n]] * (psize // TILE), axis=1)
-            message = message + column * dot(mixed, basis[n])
+            spread[:, n * psize : (n + 1) * psize] = (column * wide).astype(BF16)
+        message = dot(spread[...], basis[...])
         active = (message / (1.0 + jnp.exp(-message))).astype(BF16)
         update = dot(out_v[l].astype(F32).T.astype(BF16), active)
         hidden = (hidden.astype(F32) + update).astype(BF16)
@@ -331,7 +339,7 @@
     own = pltpu.make_async_copy(stage.at[me], force_buf.at[my_patch], local_sem.at[0])
     own.start()
 
-    lax.fori_loop(first_half, tile_count, mm_tile, 0)
+    lax.fori_loop(first_half, tile_count, mm_tile, 0, unroll=True)
 
     for copy in halo:
         copy.wait_send()
@@ -369,8 +377,8 @@
     mm_force, ml_force = pl.pallas_call(
         functools.partial(kernel, shape),
         out_shape=(
-            jax.ShapeDtypeStruct((3, count), F32),
-            jax.ShapeDtypeStruct((3, patches, atoms), F32),
+            pltpu.VMEM((3, count), F32),
+            pltpu.VMEM((3, patches, atoms), F32),
         ),
         in_specs=[ANY] * 10,
         out_specs=(VMEM, VMEM),
@@ -390,7 +398,9 @@
             pltpu.VMEM((tile_count, TILE, 32), BF16),
             pltpu.VMEM((nbrs, psize), jnp.int32),
             pltpu.VMEM((nbrs, psize), jnp.int32),
-            pltpu.VMEM((nb, psize, psize), BF16),
+            pltpu.VMEM((psize // 4, TILE), jnp.int32),
+            pltpu.VMEM((nb * psize, psize), BF16),
+            pltpu.VMEM((width, nb * psize), BF16),
             pltpu.VMEM((psize, psize), F32),
             pltpu.VMEM((layers, nb, width, TILE), F32),
             pltpu.VMEM((mls, 3, atoms), F32),

time: 28.1 us -> 24.5 us (0.87)
  Pallas kernels: 25.2 us -> 22.4 us
  local copies, waits for them, and re-layouts: 1.99 us -> 1.22 us
    pallas_call x1, Pallas kernels: 25.2 us -> 22.4 us  [on_device(): pl.pallas_call(functools.partial(kernel, shape), out_shape=(pltpu.VMEM((3...]
    unnamed x4 -> x2, local copies, waits for them, and re-layouts: 1.99 us -> 1.22 us
where the time goes in v2:
time: 24.5 us; the launch traced here: 24.3 us
  Pallas kernels  22.4 us (91%)
  local copies, waits for them, and re-layouts  1.22 us (5%)
  between operations  0.64 us (3%)
    pallas_call x1, Pallas kernels, on_device(): pl.pallas_call(functools.partial(kernel, shape), out_shape=(pltpu.VMEM((3...  22.4 us
    unnamed x2, local copies, waits for them, and re-layouts  1.22 us

profile of v2, /device:TPU:0, one launch (start us, length us, event | category | flops | bytes accessed | tf_op | source)
XLA Modules:
  0.0 24.3 jit_solution(6950797766311044620)
XLA Ops:
  0.6 22.4 %force_step.1 = (f32[3,2048]{1,0:T(4,128)S(1)}, f32[3,8,64]{2,1,0:T(8,128)S(1)}) custom-call(f32[3,2048]{1,0:T(4,128)} %mm_pos.1, f32[1,2048]{1,0:T(1,128)} %bitcast.6, s32[8,16]{1,0:T(8,128)} %bitcast.7, bf16[8,64,128]{2,1,0:T(8,128)(2,1)} %feat.1, f32[3,8,64]{2,1,0:T(8,128)} %bitcast.5, s32[8,32,64]{2,1,0:T(8,128)} %nbr.1, bf16[2,128,128]{2,1,0:T(8,128)(2,1)} %msg_w.1, ...), custom_call_target="tpu_custom_call" | custom-call | tf_op jit(solution)/shard_map/force_step/pallas_call | solution.py:377
  23.1 0.6 %copy.14 = f32[3,2048]{1,0:T(4,128)} copy(f32[3,2048]{1,0:T(4,128)S(1)} %get-tuple-element.6) | data formatting | bytes 49152
  23.7 0.6 %copy.15 = f32[8,3,64]{2,0,1:T(8,128)} copy(f32[8,3,64]{2,0,1:T(8,128)S(1)} %bitcast.4) | data formatting | bytes 12288

commit v3 on v2

--- a/solution.py
+++ b/solution.py
@@ -13,6 +13,7 @@
 SOFTEN = 1.0
 COULOMB = 0.5
 CHUNK = 32
+WAVE = (0.261799388, -0.00299057413, 1.02484123e-05, -1.67106067e-08, 1.52995984e-11)
 F32 = jnp.float32
 BF16 = jnp.bfloat16
 MESH = pl.DeviceIdType.MESH
@@ -81,13 +82,12 @@
     return jnp.dot(a, b, preferred_element_type=F32)
 
 
-def half_wave(u):
-    x = u * (math.pi / 2)
-    y = x * x
-    p = -1.0 / 39916800
-    for c in (1.0 / 362880, -1.0 / 5040, 1.0 / 120, -1.0 / 6, 1.0):
+def half_wave(w):
+    y = w * w
+    p = WAVE[-1]
+    for c in WAVE[-2::-1]:
         p = p * y + c
-    return p * x
+    return p * w
 
 
 def kernel(
@@ -186,8 +186,6 @@
                     device_id_type=MESH,
                 )
             )
-    for copy in halo:
-        copy.start()
     moves = []
     for m, (src, dst) in enumerate(((nbr, nbr_buf), (pos, pos_buf), (feat, feat_buf))):
         group = []
@@ -205,6 +203,8 @@
         for copy in group:
             copy.start()
         moves.append(group)
+    for copy in halo:
+        copy.start()
 
     for copy in local:
         copy.wait()
@@ -230,10 +230,6 @@
             near_r[slab * tile_count + t] = rows[:, t * TILE : (t + 1) * TILE]
 
     near_slab(1)
-    for copy in halo:
-        copy.wait_recv()
-    near_slab(0)
-    near_slab(2)
 
     def mm_tile(t, carry):
         own = own_u[t]
@@ -253,35 +249,40 @@
         mm_out[:, at] = force * (COULOMB * win_q[1, :, at])
         return carry
 
-    first_half = tile_count // 2
-    lax.fori_loop(0, first_half, mm_tile, 0, unroll=True)
-
     for copy in moves[0] + moves[1]:
         copy.wait_recv()
     listed = jnp.concatenate([nbr_buf[d] for d in range(mls)], axis=1)
     words = psize // 4
-    word_s[...] = lax.rem(listed, words)
-    value_s[...] = jnp.left_shift(1, 8 * (listed // words))
+    half = psize // 8
+    word_s[...] = lax.rem(listed, half)
+    value_s[...] = jnp.left_shift(1, 4 * (listed // half))
     xyz = jnp.concatenate([pos_buf[d, :, my_patch, :] for d in range(mls)], axis=1)
     senders = left_factor(xyz).T.astype(BF16)
     receivers = right_factor(xyz)
     rows = moment_rows(xyz, jnp.ones_like(xyz[0:1]))
+    weight_s[...] = dot(senders, receivers)
     for ib in range(psize // TILE):
         at = slice(ib * TILE, (ib + 1) * TILE)
-        place = lax.broadcasted_iota(jnp.int32, (words, TILE), 0)
-        counts = jnp.zeros((words, TILE), jnp.int32)
-        for k in range(nbrs):
-            hit = place == word_s[k : k + 1, at]
-            counts = counts + jnp.where(hit, value_s[k : k + 1, at], 0)
-        count_s[...] = counts
+        place = lax.broadcasted_iota(jnp.int32, (words // 2, TILE), 0)
+        even = jnp.zeros((words // 2, TILE), jnp.int32)
+        odd = even
+        for first in range(0, nbrs, 15):
+            counts = jnp.zeros((words // 2, TILE), jnp.int32)
+            for k in range(first, min(first + 15, nbrs)):
+                hit = place == word_s[k : k + 1, at]
+                counts = counts + jnp.where(hit, value_s[k : k + 1, at], 0)
+            even = even + (counts & 0x0F0F0F0F)
+            odd = odd + (jnp.right_shift(counts, 4) & 0x0F0F0F0F)
+        count_s[: words // 2] = even
+        count_s[words // 2 :] = odd
         for b in range(4):
             for c in range(0, words, CHUNK):
                 row = b * words + c
                 rows_at = slice(row, row + CHUNK)
                 count = (jnp.right_shift(count_s[c : c + CHUNK], 8 * b) & 255).astype(F32)
-                squared = dot(senders[rows_at], receivers[:, at])
+                squared = weight_s[rows_at, at]
                 distance = jnp.minimum(squared * lax.rsqrt(squared), RADIUS)
-                wave = half_wave(1.0 - distance * (1.0 / RADIUS))
+                wave = half_wave(RADIUS - distance)
                 weight = count * (wave * wave)
                 weight_s[rows_at, at] = weight
                 shifted = distance - center * step
@@ -339,7 +340,11 @@
     own = pltpu.make_async_copy(stage.at[me], force_buf.at[my_patch], local_sem.at[0])
     own.start()
 
-    lax.fori_loop(first_half, tile_count, mm_tile, 0, unroll=True)
+    for copy in halo:
+        copy.wait_recv()
+    near_slab(0)
+    near_slab(2)
+    lax.fori_loop(0, tile_count, mm_tile, 0, unroll=True)
 
     for copy in halo:
         copy.wait_send()
@@ -351,6 +356,17 @@
         copy.wait()
     for p in range(patches):
         ml_out[:, p, :] = force_buf[p]
+
+
+def finish(mm_src, ml_src, mm_dst, ml_dst, sem):
+    copies = [
+        pltpu.make_async_copy(mm_src, mm_dst, sem.at[0]),
+        pltpu.make_async_copy(ml_src, ml_dst, sem.at[1]),
+    ]
+    for copy in copies:
+        copy.start()
+    for copy in copies:
+        copy.wait()
 
 
 def on_device(
@@ -429,6 +445,17 @@
         out_weight,
         read_weight,
     )
+    mm_force, ml_force = pl.pallas_call(
+        finish,
+        out_shape=(
+            jax.ShapeDtypeStruct((3, count), F32),
+            jax.ShapeDtypeStruct((3, patches, atoms), F32),
+        ),
+        in_specs=[VMEM, VMEM],
+        out_specs=(ANY, ANY),
+        scratch_shapes=[dma((2,))],
+        name="write_out",
+    )(mm_force, ml_force)
     return mm_force, ml_force.transpose(1, 0, 2)
 
 

time: 24.5 us -> 24.5 us (level)
  the two profiles are of different devices: /device:TPU:0 before, /device:TPU:5 now
where the time goes in v3:
time: 24.5 us; the launch traced here: 24.3 us
  Pallas kernels  22.5 us (92%)
  local copies, waits for them, and re-layouts  1.19 us (5%)
  between operations  0.65 us (3%)
    pallas_call x1, Pallas kernels, on_device(): pl.pallas_call(functools.partial(kernel, shape), out_shape=(pltpu.VMEM((3...  21.1 us
    pallas_call x1, Pallas kernels, on_device(): pl.pallas_call(finish, out_shape=(jax.ShapeDtypeStruct((3, count), F32),...  1.39 us
    unnamed x4, local copies, waits for them, and re-layouts  1.19 us

profile of v3, /device:TPU:5, one launch (start us, length us, event | category | flops | bytes accessed | tf_op | source)
XLA Modules:
  0.0 24.3 jit_solution(4510851442082044615)
XLA Ops:
  0.6 21.1 %force_step.1 = (f32[3,2048]{1,0:T(4,128)S(1)}, f32[3,8,64]{2,1,0:T(8,128)S(1)}) custom-call(f32[3,2048]{1,0:T(4,128)} %mm_pos.1, f32[1,2048]{1,0:T(1,128)} %bitcast.5, s32[8,16]{1,0:T(8,128)} %bitcast.6, bf16[8,64,128]{2,1,0:T(8,128)(2,1)} %feat.1, f32[3,8,64]{2,1,0:T(8,128)} %bitcast.4, s32[8,32,64]{2,1,0:T(8,128)} %nbr.1, bf16[2,128,128]{2,1,0:T(8,128)(2,1)} %msg_w.1, ...), custom_call_target="tpu_custom_call" | custom-call | tf_op jit(solution)/shard_map/force_step/pallas_call | solution.py:393
  21.7 0.0 copy-start
  21.7 0.6 %copy-done = f32[3,2048]{1,0:T(4,128)} copy-done((f32[3,2048]{1,0:T(4,128)}, f32[3,2048]{1,0:T(4,128)S(1)}, u32[]{:S(2)}) %copy-start) | copy-done | bytes 24600
  22.3 0.0 copy-start.1
  22.3 0.6 %copy-done.1 = f32[3,8,64]{2,1,0:T(8,128)} copy-done((f32[3,8,64]{2,1,0:T(8,128)}, f32[3,8,64]{2,1,0:T(8,128)S(1)}, u32[]{:S(2)}) %copy-start.1) | copy-done | bytes 6168
  22.9 1.4 %write_out.1 = (f32[3,2048]{1,0:T(4,128)}, f32[3,8,64]{2,1,0:T(8,128)}) custom-call(f32[3,2048]{1,0:T(4,128)} %copy-done, f32[3,8,64]{2,1,0:T(8,128)} %copy-done.1), custom_call_target="tpu_custom_call" | custom-call | tf_op jit(solution)/shard_map/write_out/pallas_call | solution.py:448
Async XLA Ops:
  21.7 0.6 %copy-start = (f32[3,2048]{1,0:T(4,128)}, f32[3,2048]{1,0:T(4,128)S(1)}, u32[]{:S(2)}) copy-start(f32[3,2048]{1,0:T(4,128)S(1)} %get-tuple-element.6.mm_src) | copy-start | bytes 73732
  22.3 0.6 %copy-start.1 = (f32[3,8,64]{2,1,0:T(8,128)}, f32[3,8,64]{2,1,0:T(8,128)S(1)}, u32[]{:S(2)}) copy-start(f32[3,8,64]{2,1,0:T(8,128)S(1)} %get-tuple-element.7.ml_src) | copy-start | bytes 18436

commit v4 on v3

--- a/solution.py
+++ b/solution.py
@@ -108,8 +108,10 @@
     win_q,
     tiles,
     feat_buf,
-    pos_buf,
-    nbr_buf,
+    nbr_own,
+    pos_own,
+    geo_own,
+    geo_buf,
     msg_v,
     rad_v,
     out_v,
@@ -150,6 +152,10 @@
     sides = [(before // mls, lax.rem(before, mls)), (after // mls, lax.rem(after, mls))]
     my_patch = lax.rem(me, patches)
 
+    loads = [
+        pltpu.make_async_copy(nbr, nbr_own, local_sem.at[7]),
+        pltpu.make_async_copy(pos, pos_own, local_sem.at[8]),
+    ]
     local = [
         pltpu.make_async_copy(mm_pos, win_p.at[1], local_sem.at[0]),
         pltpu.make_async_copy(mm_charge, win_q.at[1], local_sem.at[1]),
@@ -158,11 +164,9 @@
         pltpu.make_async_copy(rad_w, rad_v, local_sem.at[4]),
         pltpu.make_async_copy(out_w, out_v, local_sem.at[5]),
         pltpu.make_async_copy(read_w, read_v, local_sem.at[6]),
-        pltpu.make_async_copy(nbr.at[my_patch], nbr_buf.at[me], local_sem.at[7]),
-        pltpu.make_async_copy(pos, pos_buf.at[me], local_sem.at[8]),
         pltpu.make_async_copy(feat.at[my_patch], feat_buf.at[me], local_sem.at[9]),
     ]
-    for copy in local:
+    for copy in loads + local:
         copy.start()
 
     barrier = pltpu.get_barrier_semaphore()
@@ -171,6 +175,19 @@
     peers = [lax.rem(me + o, mls) for o in range(1, mls)]
     for peer in peers:
         pl.semaphore_signal(barrier, inc=1, device_id=(dom, peer), device_id_type=MESH)
+
+    for copy in loads:
+        copy.wait()
+    quarter = nbrs // 4
+    assert nbrs % 4 == 0 and psize & (psize - 1) == 0 and psize <= 4096
+    for p in range(patches):
+        pairs = nbr_own[p, : 2 * quarter] + psize * nbr_own[p, 2 * quarter :]
+        pairs = jnp.concatenate([pairs[:quarter], pairs[quarter:]], axis=1)
+        geo_own[p, :quarter] = pairs.astype(F32)
+        geo_own[p, quarter : quarter + 3, :atoms] = pos_own[:, p, :]
+        geo_own[p, quarter : quarter + 3, atoms:] = pos_own[:, p, :]
+        geo_own[p, quarter + 3 :] = jnp.zeros((geo_own.shape[1] - quarter - 3, 2 * atoms), F32)
+
     pl.semaphore_wait(barrier, mls + 1)
 
     halo = []
@@ -187,12 +204,12 @@
                 )
             )
     moves = []
-    for m, (src, dst) in enumerate(((nbr, nbr_buf), (pos, pos_buf), (feat, feat_buf))):
+    for m, (src, dst) in enumerate(((geo_own, geo_buf), (feat, feat_buf))):
         group = []
         for o, peer in enumerate(peers):
             group.append(
                 pltpu.make_async_remote_copy(
-                    src_ref=src if m == 1 else src.at[lax.rem(peer, patches)],
+                    src_ref=src.at[lax.rem(peer, patches)],
                     dst_ref=dst.at[me],
                     send_sem=ml_send.at[m, o],
                     recv_sem=ml_recv.at[m, o],
@@ -206,6 +223,7 @@
     for copy in halo:
         copy.start()
 
+    geo_buf[me] = geo_own[my_patch]
     for copy in local:
         copy.wait()
     center = nb // 2
@@ -249,14 +267,23 @@
         mm_out[:, at] = force * (COULOMB * win_q[1, :, at])
         return carry
 
-    for copy in moves[0] + moves[1]:
+    for copy in moves[0]:
         copy.wait_recv()
-    listed = jnp.concatenate([nbr_buf[d] for d in range(mls)], axis=1)
+    pieces = [geo_buf[d] for d in range(mls)]
+    pairs = jnp.concatenate(
+        [
+            jnp.concatenate([piece[:quarter, :atoms] for piece in pieces], axis=1),
+            jnp.concatenate([piece[:quarter, atoms:] for piece in pieces], axis=1),
+        ],
+        axis=0,
+    ).astype(jnp.int32)
+    bits = psize.bit_length() - 1
+    listed = jnp.concatenate([pairs & (psize - 1), jnp.right_shift(pairs, bits)], axis=0)
     words = psize // 4
     half = psize // 8
-    word_s[...] = lax.rem(listed, half)
-    value_s[...] = jnp.left_shift(1, 4 * (listed // half))
-    xyz = jnp.concatenate([pos_buf[d, :, my_patch, :] for d in range(mls)], axis=1)
+    word_s[...] = listed & (half - 1)
+    value_s[...] = jnp.left_shift(1, 4 * jnp.right_shift(listed, bits - 3))
+    xyz = jnp.concatenate([piece[quarter : quarter + 3, :atoms] for piece in pieces], axis=1)
     senders = left_factor(xyz).T.astype(BF16)
     receivers = right_factor(xyz)
     rows = moment_rows(xyz, jnp.ones_like(xyz[0:1]))
@@ -300,7 +327,7 @@
                     value = value * down
                     basis[n * psize + row : n * psize + row + CHUNK, at] = value.astype(BF16)
 
-    for copy in moves[2]:
+    for copy in moves[1]:
         copy.wait_recv()
     hidden = feat_buf[...].reshape(psize, width).astype(F32).T.astype(BF16)
     for l in range(layers):
@@ -358,17 +385,6 @@
         ml_out[:, p, :] = force_buf[p]
 
 
-def finish(mm_src, ml_src, mm_dst, ml_dst, sem):
-    copies = [
-        pltpu.make_async_copy(mm_src, mm_dst, sem.at[0]),
-        pltpu.make_async_copy(ml_src, ml_dst, sem.at[1]),
-    ]
-    for copy in copies:
-        copy.start()
-    for copy in copies:
-        copy.wait()
-
-
 def on_device(
     shape,
     mm_positions,
@@ -390,6 +406,7 @@
     count = mm_positions.shape[1]
     tile_count = count // TILE
     dma = pltpu.SemaphoreType.DMA
+    geo_rows = (nbrs // 4 + 3 + 7) // 8 * 8
     mm_force, ml_force = pl.pallas_call(
         functools.partial(kernel, shape),
         out_shape=(
@@ -403,8 +420,10 @@
             pltpu.VMEM((3, 1, count), F32),
             pltpu.SMEM(mm_tiles.shape[::-1], jnp.int32),
             pltpu.VMEM((mls, atoms, width), BF16),
-            pltpu.VMEM((mls, 3, patches, atoms), F32),
-            pltpu.VMEM((mls, nbrs, atoms), jnp.int32),
+            pltpu.VMEM((patches, nbrs, atoms), jnp.int32),
+            pltpu.VMEM((3, patches, atoms), F32),
+            pltpu.VMEM((patches, geo_rows, 2 * atoms), F32),
+            pltpu.VMEM((mls, geo_rows, 2 * atoms), F32),
             pltpu.VMEM(msg_weight.shape, BF16),
             pltpu.VMEM(radial_weight.shape, F32),
             pltpu.VMEM(out_weight.shape, BF16),
@@ -424,8 +443,8 @@
             dma((10,)),
             dma((4,)),
             dma((4,)),
-            dma((3, mls)),
-            dma((3, mls)),
+            dma((2, mls)),
+            dma((2, mls)),
             dma((patches,)),
             dma((patches,)),
         ],
@@ -445,17 +464,6 @@
         out_weight,
         read_weight,
     )
-    mm_force, ml_force = pl.pallas_call(
-        finish,
-        out_shape=(
-            jax.ShapeDtypeStruct((3, count), F32),
-            jax.ShapeDtypeStruct((3, patches, atoms), F32),
-        ),
-        in_specs=[VMEM, VMEM],
-        out_specs=(ANY, ANY),
-        scratch_shapes=[dma((2,))],
-        name="write_out",
-    )(mm_force, ml_force)
     return mm_force, ml_force.transpose(1, 0, 2)
 
 

time: 24.5 us -> 21.6 us (0.88)
  the two profiles are of different devices: /device:TPU:5 before, /device:TPU:7 now
where the time goes in v4:
time: 21.6 us; the launch traced here: 21.5 us
  Pallas kernels  19.6 us (91%)
  local copies, waits for them, and re-layouts  1.22 us (6%)
  between operations  0.64 us (3%)
    pallas_call x1, Pallas kernels, on_device(): pl.pallas_call(functools.partial(kernel, shape), out_shape=(pltpu.VMEM((3...  19.6 us
    unnamed x2, local copies, waits for them, and re-layouts  1.22 us

profile of v4, /device:TPU:7, one launch (start us, length us, event | category | flops | bytes accessed | tf_op | source)
XLA Modules:
  0.0 21.5 jit_solution(13816385991096822379)
XLA Ops:
  0.6 19.6 %force_step.1 = (f32[3,2048]{1,0:T(4,128)S(1)}, f32[3,8,64]{2,1,0:T(8,128)S(1)}) custom-call(f32[3,2048]{1,0:T(4,128)} %mm_pos.1, f32[1,2048]{1,0:T(1,128)} %bitcast.6, s32[8,16]{1,0:T(8,128)} %bitcast.7, bf16[8,64,128]{2,1,0:T(8,128)(2,1)} %feat.1, f32[3,8,64]{2,1,0:T(8,128)} %bitcast.5, s32[8,32,64]{2,1,0:T(8,128)} %nbr.1, bf16[2,128,128]{2,1,0:T(8,128)(2,1)} %msg_w.1, ...), custom_call_target="tpu_custom_call" | custom-call | tf_op jit(solution)/shard_map/force_step/pallas_call | solution.py:410
  20.3 0.6 %copy.14 = f32[3,2048]{1,0:T(4,128)} copy(f32[3,2048]{1,0:T(4,128)S(1)} %get-tuple-element.6) | data formatting | bytes 49152
  20.9 0.6 %copy.15 = f32[8,3,64]{2,0,1:T(8,128)} copy(f32[8,3,64]{2,0,1:T(8,128)S(1)} %bitcast.4) | data formatting | bytes 12288
